TPU v7x, 256 devices: a whole 4x4x8 slice. The times are simulated.
256 devices in a mesh: dp: 16 (over y, x), seq: 16 (over z, core).
Axes of the slice: x: 4, y: 4, z: 8, core: 2. Of those that a mesh axis runs over, the one named last changes fastest.
Arguments:
- queries: bfloat16 [32768, 8192], P(('dp', 'seq')), parts along dimension 0, may hold values from -7 to 7
- key_rows: bfloat16 [32768, 1024], P(('dp', 'seq')), parts along dimension 0, may hold values from -5 to 5
- value_rows: bfloat16 [32768, 1024], P(('dp', 'seq')), parts along dimension 0, may hold values from -6 to 6
- outputs: bfloat16 [32768, 8192], P(('dp', 'seq')), parts along dimension 0, may hold values from -3 to 3
- out_grads: bfloat16 [32768, 8192], P(('dp', 'seq')), parts along dimension 0, may hold values from -1.5 to 1.5
- log_normalizer: float32 [32768, 64], P(('dp', 'seq')), parts along dimension 0, may hold values from -30 to 40, as said below
- doc_starts: int32 [128], P('dp'), parts along dimension 0, may hold values from 0 to 2047, as said below
- doc_weights: float32 [128], P('dp'), parts along dimension 0, may hold values from 0.25 to 2.5
Outputs:
- query_grads: bfloat16 [32768, 8192], P(('dp', 'seq')), parts along dimension 0
- key_grads: bfloat16 [32768, 1024], P(('dp', 'seq')), parts along dimension 0
- value_grads: bfloat16 [32768, 1024], P(('dp', 'seq')), parts along dimension 0
There are 16 independent parts, one for each index of `dp`. A program takes and returns all parts, laid end to end along the dimension named above; each array names one. Nothing has to cross between parts.
Inputs may be any that keep to these rules, and one draw needn't show every extreme that they name: `doc_starts`: 8 documents in order: starts rise from 0, each document runs to the next start or to the end of the window, is 1 to 512 tokens long, and one is exactly 512 long. `log_normalizer`: the log of the sum of exp(scores) over the allowed keys of each token and head.
All inputs are finite; a program needn't handle non-finite values.
Results may differ from a plain program's by a relative error of at most 0.0049.
Values may be sent and summed in bfloat16 or wider, within the bound.
A program may use at most 128 MiB of HBM per device.

v0:
```python
import jax
import jax.numpy as jnp
from jax import lax
from jax.sharding import PartitionSpec as P

HEADS = 64
KVH = 8
HD = 128


def per_device(
    queries, key_rows, value_rows, outputs, out_grads, log_normalizer, doc_starts, doc_weights
):
    seq_count = lax.axis_size("seq")
    tok_dev = queries.shape[0]
    repeat = seq_count // KVH
    heads_here = HEADS // seq_count

    def spread(block):
        widened = jnp.broadcast_to(block.reshape(tok_dev, KVH, 1, HD), (tok_dev, KVH, repeat, HD))
        return widened.reshape(tok_dev, seq_count * HD)

    keys_wide = spread(key_rows)
    values_wide = spread(value_rows)
    query_all, key_all, value_all, grad_all, output_all = (
        lax.all_to_all(queries, "seq", split_axis=1, concat_axis=0, tiled=True),
        lax.all_to_all(keys_wide, "seq", split_axis=1, concat_axis=0, tiled=True),
        lax.all_to_all(values_wide, "seq", split_axis=1, concat_axis=0, tiled=True),
        lax.all_to_all(out_grads, "seq", split_axis=1, concat_axis=0, tiled=True),
        lax.all_to_all(outputs, "seq", split_axis=1, concat_axis=0, tiled=True),
    )
    norm_all = lax.all_to_all(log_normalizer, "seq", split_axis=1, concat_axis=0, tiled=True)
    product = grad_all.astype(jnp.float32) * output_all.astype(jnp.float32)
    delta_all = jnp.sum(product.reshape(query_all.shape[0], heads_here, HD), axis=-1)
    window = query_all.shape[0]
    query_heads = query_all.reshape(window, heads_here, HD)
    grad_heads = grad_all.reshape(window, heads_here, HD)
    positions = jnp.arange(window, dtype=jnp.int32)
    doc_of = jnp.sum((positions[:, None] >= doc_starts[None, :]).astype(jnp.int32), axis=1) - 1
    member = doc_of[:, None] == jnp.arange(doc_starts.shape[0], dtype=jnp.int32)[None, :]
    row_weight = jnp.sum(
        jnp.where(member, doc_weights[None, :], jnp.zeros((), jnp.float32)), axis=1
    )
    tile_rows = window // 8
    reach = (window // 4 - 1 + tile_rows - 1) // tile_rows
    score_scale = HD ** (-0.5)
    key_blocks = [jnp.zeros((tile_rows, HD), jnp.float32) for block_index in range(8)]
    value_blocks = [jnp.zeros((tile_rows, HD), jnp.float32) for block_index in range(8)]
    query_blocks = []
    for row_block in range(8):
        row_start = row_block * tile_rows
        query_tile = query_heads[row_start : row_start + tile_rows]
        grad_tile = grad_heads[row_start : row_start + tile_rows]
        norm_tile = norm_all[row_start : row_start + tile_rows].T
        delta_tile = delta_all[row_start : row_start + tile_rows].T
        weight_tile = row_weight[row_start : row_start + tile_rows]
        doc_rows = doc_of[row_start : row_start + tile_rows]
        pos_rows = positions[row_start : row_start + tile_rows]
        block_list = list(range(max(0, row_block - reach), row_block + 1))

        def tile_scores(key_block):
            key_start = key_block * tile_rows
            key_tile = key_all[key_start : key_start + tile_rows]
            scores = (
                jnp.einsum("qhd,kd->hqk", query_tile, key_tile, preferred_element_type=jnp.float32)
                * score_scale
            )
            same_doc = doc_rows[:, None] == doc_of[key_start : key_start + tile_rows][None, :]
            causal = positions[key_start : key_start + tile_rows][None, :] <= pos_rows[:, None]
            probs = jnp.where(
                (same_doc & causal)[None],
                jnp.exp(scores - norm_tile[:, :, None]),
                jnp.zeros((), jnp.float32),
            )
            return (scores, probs)

        def tile_mean(key_block):
            scores, probs = tile_scores(key_block)
            return jnp.sum(probs * scores, axis=-1)

        def tile_grads(key_block, mean_score):
            scores, probs = tile_scores(key_block)
            key_start = key_block * tile_rows
            key_tile = key_all[key_start : key_start + tile_rows]
            value_tile = value_all[key_start : key_start + tile_rows]
            prob_grads = jnp.einsum(
                "qhd,kd->hqk", grad_tile, value_tile, preferred_element_type=jnp.float32
            )
            score_grads = probs * (
                prob_grads
                - delta_tile[:, :, None]
                - weight_tile[None, :, None] * (scores - mean_score[:, :, None])
            )
            score_low = score_grads.astype(jnp.bfloat16)
            probs_low = probs.astype(jnp.bfloat16)
            query_term = jnp.einsum(
                "hqk,kd->qhd", score_low, key_tile, preferred_element_type=jnp.float32
            )
            key_term = jnp.einsum(
                "hqk,qhd->kd", score_low, query_tile, preferred_element_type=jnp.float32
            )
            value_term = jnp.einsum(
                "hqk,qhd->kd", probs_low, grad_tile, preferred_element_type=jnp.float32
            )
            return (query_term, key_term, value_term)

        mean_score = jnp.zeros((heads_here, tile_rows), jnp.float32)
        for key_block in block_list:
            mean_score = mean_score + tile_mean(key_block)
        query_acc = jnp.zeros((tile_rows, heads_here, HD), jnp.float32)
        for key_block in block_list:
            terms = tile_grads(key_block, mean_score)
            query_acc = query_acc + terms[0]
            key_blocks[key_block] = key_blocks[key_block] + terms[1]
            value_blocks[key_block] = value_blocks[key_block] + terms[2]
        query_blocks.append(
            (query_acc * score_scale).astype(jnp.bfloat16).reshape(tile_rows, heads_here * HD)
        )
    query_full = jnp.concatenate(query_blocks, axis=0)
    key_part = jnp.concatenate(key_blocks, axis=0) * score_scale
    value_part = jnp.concatenate(value_blocks, axis=0)
    query_grads = lax.all_to_all(query_full, "seq", split_axis=0, concat_axis=1, tiled=True)
    partials = jnp.concatenate([key_part, value_part], axis=1)
    arrived = lax.all_to_all(partials, "seq", split_axis=0, concat_axis=1, tiled=True)
    summed = jnp.sum(arrived.reshape(tok_dev, KVH, repeat, 2, HD), axis=2).astype(jnp.bfloat16)
    key_grads = summed[:, :, 0, :].reshape(tok_dev, KVH * HD)
    value_grads = summed[:, :, 1, :].reshape(tok_dev, KVH * HD)
    return (query_grads, key_grads, value_grads)


def solution(mesh):
    in_specs = (
        P(("dp", "seq"), None),
        P(("dp", "seq"), None),
        P(("dp", "seq"), None),
        P(("dp", "seq"), None),
        P(("dp", "seq"), None),
        P(("dp", "seq"), None),
        P("dp"),
        P("dp"),
    )
    out_specs = (P(("dp", "seq"), None), P(("dp", "seq"), None), P(("dp", "seq"), None))
    return jax.shard_map(
        per_device, mesh=mesh, in_specs=in_specs, out_specs=out_specs, check_vma=False
    )
```

profile of v0, /device:TPU:1, one launch (start us, length us, event | category | flops | bytes accessed | tf_op | source)
XLA Modules:
  0.0 493.0 jit_solution(6301434196638950427)
XLA Ops:
  0.7 10.1 %all-to-all-start.2 = ((f32[128,16,4]{0,2,1:T(4,128)}), f32[128,16,4]{0,2,1:T(4,128)S(1)}, u32[]{:S(2)}, u32[]{:S(2)}) async-start(f32[128,16,4]{0,2,1:T(4,128)} %bitcast.791), calls=%async_computation.2 | async-start | bytes 65536 | tf_op jit(solution)/shard_map/all_to_all | solution.py:32
  10.9 7.3 %all-to-all-done.2 = f32[128,16,4]{0,2,1:T(4,128)S(1)} async-done(((f32[128,16,4]{0,2,1:T(4,128)}), f32[128,16,4]{0,2,1:T(4,128)S(1)}, u32[]{:S(2)}, u32[]{:S(2)}) %all-to-all-start.2) | async-done | bytes 32800 | tf_op jit(solution)/shard_map/all_to_all | solution.py:32
  19.1 3.8 all-to-all-start
  22.9 17.3 %all-to-all-done = bf16[128,16,128]{2,0,1:T(8,128)(2,1)S(1)} async-done(((bf16[128,16,128]{2,0,1:T(8,128)(2,1)}), bf16[128,16,128]{2,0,1:T(8,128)(2,1)S(1)}, u32[]{:S(2)}, u32[]{:S(2)}) %all-to-all-start) | async-done | bytes 524320 | tf_op jit(solution)/shard_map/all_to_all | solution.py:27
  41.1 4.1 all-to-all-start.3
  46.8 14.6 %all-to-all-done.3 = bf16[128,16,128]{2,0,1:T(8,128)(2,1)} async-done(((bf16[128,16,128]{2,0,1:T(8,128)(2,1)}), bf16[128,16,128]{2,0,1:T(8,128)(2,1)}, u32[]{:S(2)}, u32[]{:S(2)}) %all-to-all-start.3) | async-done | bytes 524320 | tf_op jit(solution)/shard_map/all_to_all | solution.py:28
  61.4 3.6 all-to-all-start.1
  65.0 3.1 copy.865
  68.2 45.1 %all-to-all-done.1 = bf16[128,16,512]{2,0,1:T(8,128)(2,1)S(1)} async-done(((bf16[128,16,512]{2,0,1:T(8,128)(2,1)}), bf16[128,16,512]{2,0,1:T(8,128)(2,1)S(1)}, u32[]{:S(2)}, u32[]{:S(2)}) %all-to-all-start.1) | async-done | bytes 2097184 | tf_op jit(solution)/shard_map/all_to_all | solution.py:26
  114.6 5.0 %all-to-all-start.5 = ((bf16[128,16,512]{2,0,1:T(8,128)(2,1)}), bf16[128,16,512]{2,0,1:T(8,128)(2,1)}, u32[]{:S(2)}, u32[]{:S(2)}) async-start(bf16[128,16,512]{2,0,1:T(8,128)(2,1)} %bitcast.707), calls=%async_computation.5 | async-start | bytes 4194304 | tf_op jit(solution)/shard_map/all_to_all | solution.py:30
  119.6 3.2 copy.866
  122.8 45.9 %all-to-all-done.5 = bf16[128,16,512]{2,0,1:T(8,128)(2,1)} async-done(((bf16[128,16,512]{2,0,1:T(8,128)(2,1)}), bf16[128,16,512]{2,0,1:T(8,128)(2,1)}, u32[]{:S(2)}, u32[]{:S(2)}) %all-to-all-start.5) | async-done | bytes 2097184 | tf_op jit(solution)/shard_map/all_to_all | solution.py:30
  168.7 5.1 %all-to-all-start.4 = ((bf16[128,16,512]{2,0,1:T(8,128)(2,1)}), bf16[128,16,512]{2,0,1:T(8,128)(2,1)S(1)}, u32[]{:S(2)}, u32[]{:S(2)}) async-start(bf16[128,16,512]{2,0,1:T(8,128)(2,1)} %bitcast.703), calls=%async_computation.4 | async-start | bytes 4194304 | tf_op jit(solution)/shard_map/all_to_all | solution.py:29
  174.7 2.6 compare_and_fusion.2
  184.5 38.3 %all-to-all-done.4 = bf16[128,16,512]{2,0,1:T(8,128)(2,1)S(1)} async-done(((bf16[128,16,512]{2,0,1:T(8,128)(2,1)}), bf16[128,16,512]{2,0,1:T(8,128)(2,1)S(1)}, u32[]{:S(2)}, u32[]{:S(2)}) %all-to-all-start.4) | async-done | bytes 2097184 | tf_op jit(solution)/shard_map/all_to_all | solution.py:29
  222.7 4.2 bitcast_multiply_fusion
  227.0 5.2 %reshape.1343 = f32[2048,4,128]{2,1,0:T(4,128)} reshape(f32[16,128,512]{2,1,0:T(8,128)} %bitcast_multiply_fusion) | data formatting | bytes 8388608 | tf_op jit(solution)/shard_map/mul | solution.py:33
  232.2 5.2 %reduce_sum.226 = f32[2048,4]{1,0:T(8,128)S(1)} reduce(f32[2048,4,128]{2,1,0:T(4,128)} %reshape.1343, f32[]{:T(128)} %constant.2.clone.1), dimensions={2}, to_apply=%region_1.0 | reduce | flops 1040384 | bytes 4227076 | tf_op jit(solution)/shard_map/reduce_sum | solution.py:34
  241.2 2.4 convolution_bitcast_fusion.36
  243.6 3.3 multiply_reduce_fusion.13
  251.5 2.3 convolution_bitcast_fusion.39
  253.8 2.3 multiply_reduce_fusion.16
  263.3 3.1 multiply_reduce_fusion.18
  276.1 2.3 convolution_bitcast_fusion.33
  278.5 2.3 multiply_reduce_fusion.10
  289.2 2.3 convolution_bitcast_fusion.30
  291.5 2.7 multiply_reduce_fusion.7
  302.9 2.3 convolution_bitcast_fusion.27
  305.2 2.7 multiply_reduce_fusion.4
  314.3 2.1 fusion.66
  318.1 2.3 convolution_bitcast_fusion.24
  320.5 2.7 multiply_reduce_fusion.1
  329.3 2.3 fusion.86
  332.6 2.1 convolution_bitcast_fusion.45
  334.7 2.0 convolution_bitcast_fusion.43
  359.8 3.4 fusion.122
  363.3 3.4 fusion.127
  366.8 2.1 fusion.130
  368.9 2.1 fusion.133
  378.7 5.1 %all-to-all-start.7 = ((f32[16,128,256]{2,1,0:T(8,128)}), f32[16,128,256]{2,1,0:T(8,128)S(1)}, u32[]{:S(2)}, u32[]{:S(2)}) async-start(f32[16,128,256]{2,1,0:T(8,128)} %pad_maximum_fusion), calls=%async_computation.7 | async-start | bytes 4194304 | tf_op jit(solution)/shard_map/all_to_all | solution.py:124
  396.6 3.9 copy.551
  400.5 32.3 %all-to-all-done.7 = f32[16,128,256]{2,1,0:T(8,128)S(1)} async-done(((f32[16,128,256]{2,1,0:T(8,128)}), f32[16,128,256]{2,1,0:T(8,128)S(1)}, u32[]{:S(2)}, u32[]{:S(2)}) %all-to-all-start.7) | async-done | bytes 2097184 | tf_op jit(solution)/shard_map/all_to_all | solution.py:124
  432.8 5.0 %all-to-all-start.6 = ((bf16[16,128,512]{2,1,0:T(8,128)(2,1)}), bf16[16,128,512]{2,1,0:T(8,128)(2,1)}, u32[]{:S(2)}, u32[]{:S(2)}) async-start(bf16[16,128,512]{2,1,0:T(8,128)(2,1)} %bitcast.705), calls=%async_computation.6 | async-start | bytes 4194304 | tf_op jit(solution)/shard_map/all_to_all | solution.py:122
  437.8 2.1 reshape.1263
  439.9 3.3 reduce_sum.249
  446.6 40.2 %all-to-all-done.6 = bf16[16,128,512]{2,1,0:T(8,128)(2,1)} async-done(((bf16[16,128,512]{2,1,0:T(8,128)(2,1)}), bf16[16,128,512]{2,1,0:T(8,128)(2,1)}, u32[]{:S(2)}, u32[]{:S(2)}) %all-to-all-start.6) | async-done | bytes 2097184 | tf_op jit(solution)/shard_map/all_to_all | solution.py:122
  486.8 3.0 copy.552
  489.9 2.9 copy.597
  (632 shorter events, 115.3 us)
Async XLA Ops:
  0.6 10.2 %copy-start = (bf16[128,1024]{1,0:T(8,128)(2,1)S(1)}, bf16[128,1024]{1,0:T(8,128)(2,1)}, u32[]{:S(2)}) copy-start(bf16[128,1024]{1,0:T(8,128)(2,1)} %param.9) | copy-start | bytes 786436
  0.6 22.2 %copy-start.96 = (bf16[128,1024]{1,0:T(8,128)(2,1)S(1)}, bf16[128,1024]{1,0:T(8,128)(2,1)}, u32[]{:S(2)}) copy-start(bf16[128,1024]{1,0:T(8,128)(2,1)} %param.10) | copy-start | bytes 786436
  0.7 17.5 %all-to-all-start.2 = ((f32[128,16,4]{0,2,1:T(4,128)}), f32[128,16,4]{0,2,1:T(4,128)S(1)}, u32[]{:S(2)}, u32[]{:S(2)}) async-start(f32[128,16,4]{0,2,1:T(4,128)} %bitcast.791), calls=%async_computation.2 | async-start | bytes 65536 | tf_op jit(solution)/shard_map/all_to_all | solution.py:32
  10.8 34.4 %copy-start.30 = (bf16[128,8192]{1,0:T(8,128)(2,1)S(1)}, bf16[128,8192]{1,0:T(8,128)(2,1)}, u32[]{:S(2)}) copy-start(bf16[128,8192]{1,0:T(8,128)(2,1)} %param.8) | copy-start | bytes 6291460
  19.1 21.1 %all-to-all-start = ((bf16[128,16,128]{2,0,1:T(8,128)(2,1)}), bf16[128,16,128]{2,0,1:T(8,128)(2,1)S(1)}, u32[]{:S(2)}, u32[]{:S(2)}) async-start(bf16[128,16,128]{2,0,1:T(8,128)(2,1)} %bitcast.744), calls=%async_computation | async-start | bytes 1048576 | tf_op jit(solution)/shard_map/all_to_all | solution.py:27
  41.1 20.3 %all-to-all-start.3 = ((bf16[128,16,128]{2,0,1:T(8,128)(2,1)}), bf16[128,16,128]{2,0,1:T(8,128)(2,1)}, u32[]{:S(2)}, u32[]{:S(2)}) async-start(bf16[128,16,128]{2,0,1:T(8,128)(2,1)} %bitcast.745), calls=%async_computation.3 | async-start | bytes 1048576 | tf_op jit(solution)/shard_map/all_to_all | solution.py:28
  61.4 51.9 %all-to-all-start.1 = ((bf16[128,16,512]{2,0,1:T(8,128)(2,1)}), bf16[128,16,512]{2,0,1:T(8,128)(2,1)S(1)}, u32[]{:S(2)}, u32[]{:S(2)}) async-start(bf16[128,16,512]{2,0,1:T(8,128)(2,1)} %bitcast.706), calls=%async_computation.1 | async-start | bytes 4194304 | tf_op jit(solution)/shard_map/all_to_all | solution.py:26
  114.6 54.0 %all-to-all-start.5 = ((bf16[128,16,512]{2,0,1:T(8,128)(2,1)}), bf16[128,16,512]{2,0,1:T(8,128)(2,1)}, u32[]{:S(2)}, u32[]{:S(2)}) async-start(bf16[128,16,512]{2,0,1:T(8,128)(2,1)} %bitcast.707), calls=%async_computation.5 | async-start | bytes 4194304 | tf_op jit(solution)/shard_map/all_to_all | solution.py:30
  168.7 5.2 %copy-start.224 = (s32[8]{0:T(128)S(1)}, s32[8]{0:T(128)}, u32[]{:S(2)}) copy-start(s32[8]{0:T(128)} %param.14) | copy-start | bytes 100
  168.7 5.3 %copy-start.225 = (f32[8]{0:T(128)S(1)}, f32[8]{0:T(128)}, u32[]{:S(2)}) copy-start(f32[8]{0:T(128)} %param.15) | copy-start | bytes 100
  168.7 54.1 %all-to-all-start.4 = ((bf16[128,16,512]{2,0,1:T(8,128)(2,1)}), bf16[128,16,512]{2,0,1:T(8,128)(2,1)S(1)}, u32[]{:S(2)}, u32[]{:S(2)}) async-start(bf16[128,16,512]{2,0,1:T(8,128)(2,1)} %bitcast.703), calls=%async_computation.4 | async-start | bytes 4194304 | tf_op jit(solution)/shard_map/all_to_all | solution.py:29
  173.8 6.8 %copy-start.3 = (bf16[128,16,512]{2,0,1:T(8,128)(2,1)S(1)}, bf16[128,16,512]{2,0,1:T(8,128)(2,1)}, u32[]{:S(2)}) copy-start(bf16[128,16,512]{2,0,1:T(8,128)(2,1)} %copy-done.2) | copy-start | bytes 6291460
  177.9 133.7 %copy-start.166 = (f32[4,256]{1,0:T(4,128)}, f32[4,256]{1,0:T(4,128)S(1)}, u32[]{:S(2)}) copy-start(f32[4,256]{1,0:T(4,128)S(1)} %get-tuple-element.73) | copy-start | bytes 12292
  241.2 5.8 %copy-start.97 = (bf16[256,4,128]{2,1,0:T(4,128)(2,1)}, bf16[256,4,128]{2,1,0:T(4,128)(2,1)S(1)}, u32[]{:S(2)}) copy-start(bf16[256,4,128]{2,1,0:T(4,128)(2,1)S(1)} %slice.595) | copy-start | bytes 786436
  250.0 22.2 %copy-start.58 = (f32[4,256,256]{1,2,0:T(8,128)}, f32[4,256,256]{1,2,0:T(8,128)S(1)}, u32[]{:S(2)}) copy-start(f32[4,256,256]{1,2,0:T(8,128)S(1)} %fusion.81) | copy-start | bytes 3145732
  251.4 4.8 copy-start.195
  251.5 8.3 %copy-start.100 = (bf16[256,4,128]{2,1,0:T(4,128)(2,1)}, bf16[256,4,128]{2,1,0:T(4,128)(2,1)S(1)}, u32[]{:S(2)}) copy-start(bf16[256,4,128]{2,1,0:T(4,128)(2,1)S(1)} %slice.581) | copy-start | bytes 786436
  275.2 5.7 %copy-start.60 = (f32[4,256,256]{1,2,0:T(8,128)}, f32[4,256,256]{1,2,0:T(8,128)S(1)}, u32[]{:S(2)}) copy-start(f32[4,256,256]{1,2,0:T(8,128)S(1)} %fusion.75) | copy-start | bytes 3145732
  276.1 6.0 %copy-start.105 = (bf16[256,4,128]{2,1,0:T(4,128)(2,1)}, bf16[256,4,128]{2,1,0:T(4,128)(2,1)S(1)}, u32[]{:S(2)}) copy-start(bf16[256,4,128]{2,1,0:T(4,128)(2,1)S(1)} %slice.609) | copy-start | bytes 786436
  285.1 57.4 %copy-start.10 = (bf16[4,256,256]{1,2,0:T(8,128)(2,1)}, bf16[4,256,256]{1,2,0:T(8,128)(2,1)S(1)}, u32[]{:S(2)}) copy-start(bf16[4,256,256]{1,2,0:T(8,128)(2,1)S(1)} %fusion.98) | copy-start | bytes 1572868
  289.1 6.1 %copy-start.193 = (f32[256,4]{0,1:T(4,128)}, f32[256,4]{0,1:T(4,128)S(1)}, u32[]{:S(2)}) copy-start(f32[256,4]{0,1:T(4,128)S(1)} %copy.670) | copy-start | bytes 12292
  289.2 6.0 %copy-start.108 = (bf16[256,4,128]{2,1,0:T(4,128)(2,1)}, bf16[256,4,128]{2,1,0:T(4,128)(2,1)S(1)}, u32[]{:S(2)}) copy-start(bf16[256,4,128]{2,1,0:T(4,128)(2,1)S(1)} %slice.623) | copy-start | bytes 786436
  298.2 42.4 %copy-start.12 = (bf16[4,256,256]{1,2,0:T(8,128)(2,1)}, bf16[4,256,256]{1,2,0:T(8,128)(2,1)S(1)}, u32[]{:S(2)}) copy-start(bf16[4,256,256]{1,2,0:T(8,128)(2,1)S(1)} %fusion.95) | copy-start | bytes 1572868
  302.9 7.4 %copy-start.111 = (bf16[256,4,128]{2,1,0:T(4,128)(2,1)}, bf16[256,4,128]{2,1,0:T(4,128)(2,1)S(1)}, u32[]{:S(2)}) copy-start(bf16[256,4,128]{2,1,0:T(4,128)(2,1)S(1)} %slice.637) | copy-start | bytes 786436
  317.4 8.2 %copy-start.188 = (f32[256,4]{0,1:T(4,128)}, f32[256,4]{0,1:T(4,128)S(1)}, u32[]{:S(2)}) copy-start(f32[256,4]{0,1:T(4,128)S(1)} %copy.672) | copy-start | bytes 12292
  332.6 6.1 %copy-start.14 = (bf16[4,256,256]{1,2,0:T(8,128)(2,1)S(1)}, bf16[4,256,256]{1,2,0:T(8,128)(2,1)}, u32[]{:S(2)}) copy-start(bf16[4,256,256]{1,2,0:T(8,128)(2,1)} %fusion.92) | copy-start | bytes 1572868
  332.6 7.1 %copy-start.24 = (bf16[4,256,256]{1,2,0:T(8,128)(2,1)S(1)}, bf16[4,256,256]{1,2,0:T(8,128)(2,1)}, u32[]{:S(2)}) copy-start(bf16[4,256,256]{1,2,0:T(8,128)(2,1)} %fusion.96) | copy-start | bytes 1572868
  334.7 6.9 %copy-start.22 = (bf16[4,256,256]{1,2,0:T(8,128)(2,1)S(1)}, bf16[4,256,256]{1,2,0:T(8,128)(2,1)}, u32[]{:S(2)}) copy-start(bf16[4,256,256]{1,2,0:T(8,128)(2,1)} %fusion.99) | copy-start | bytes 1572868
  338.7 4.7 copy-start.18
  349.5 8.4 %copy-start.40 = (bf16[4,256,256]{1,2,0:T(8,128)(2,1)}, bf16[4,256,256]{1,2,0:T(8,128)(2,1)S(1)}, u32[]{:S(2)}) copy-start(bf16[4,256,256]{1,2,0:T(8,128)(2,1)S(1)} %fusion.106) | copy-start | bytes 1572868
  351.2 23.7 %copy-start.28 = (bf16[4,256,256]{1,2,0:T(8,128)(2,1)}, bf16[4,256,256]{1,2,0:T(8,128)(2,1)S(1)}, u32[]{:S(2)}) copy-start(bf16[4,256,256]{1,2,0:T(8,128)(2,1)S(1)} %fusion.88) | copy-start | bytes 1572868
  363.3 7.8 %copy-start.31 = (bf16[4,256,256]{1,2,0:T(8,128)(2,1)S(1)}, bf16[4,256,256]{1,2,0:T(8,128)(2,1)}, u32[]{:S(2)}) copy-start(bf16[4,256,256]{1,2,0:T(8,128)(2,1)} %fusion.100) | copy-start | bytes 1572868
  366.7 5.3 %copy-start.33 = (bf16[4,256,256]{1,2,0:T(8,128)(2,1)S(1)}, bf16[4,256,256]{1,2,0:T(8,128)(2,1)}, u32[]{:S(2)}) copy-start(bf16[4,256,256]{1,2,0:T(8,128)(2,1)} %fusion.97) | copy-start | bytes 1572868
  366.7 5.3 %copy-start.86 = (f32[256,128]{1,0:T(8,128)S(1)}, f32[256,128]{1,0:T(8,128)}, u32[]{:S(2)}) copy-start(f32[256,128]{1,0:T(8,128)} %convolution_bitcast_fusion.48) | copy-start | bytes 393220
  366.7 5.3 %copy-start.87 = (f32[256,128]{1,0:T(8,128)S(1)}, f32[256,128]{1,0:T(8,128)}, u32[]{:S(2)}) copy-start(f32[256,128]{1,0:T(8,128)} %convolution_bitcast_fusion.49) | copy-start | bytes 393220
  366.7 6.2 %copy-start.36 = (bf16[4,256,256]{1,2,0:T(8,128)(2,1)S(1)}, bf16[4,256,256]{1,2,0:T(8,128)(2,1)}, u32[]{:S(2)}) copy-start(bf16[4,256,256]{1,2,0:T(8,128)(2,1)} %fusion.94) | copy-start | bytes 1572868
  366.8 6.2 %copy-start.84 = (f32[256,128]{1,0:T(8,128)S(1)}, f32[256,128]{1,0:T(8,128)}, u32[]{:S(2)}) copy-start(f32[256,128]{1,0:T(8,128)} %convolution_bitcast_fusion.45) | copy-start | bytes 393220
  366.8 6.2 %copy-start.85 = (f32[256,128]{1,0:T(8,128)S(1)}, f32[256,128]{1,0:T(8,128)}, u32[]{:S(2)}) copy-start(f32[256,128]{1,0:T(8,128)} %convolution_bitcast_fusion.46) | copy-start | bytes 393220
  368.9 5.0 %copy-start.38 = (bf16[4,256,256]{1,2,0:T(8,128)(2,1)S(1)}, bf16[4,256,256]{1,2,0:T(8,128)(2,1)}, u32[]{:S(2)}) copy-start(bf16[4,256,256]{1,2,0:T(8,128)(2,1)} %fusion.91) | copy-start | bytes 1572868
  368.9 5.0 %copy-start.95 = (f32[256,128]{1,0:T(8,128)S(1)}, f32[256,128]{1,0:T(8,128)}, u32[]{:S(2)}) copy-start(f32[256,128]{1,0:T(8,128)} %convolution_bitcast_fusion.43) | copy-start | bytes 393220
  378.7 5.2 %copy-start.116 = (bf16[4,256,128]{1,2,0:T(8,128)(2,1)S(1)}, bf16[4,256,128]{1,2,0:T(8,128)(2,1)}, u32[]{:S(2)}) copy-start(bf16[4,256,128]{1,2,0:T(8,128)(2,1)} %fusion.122) | copy-start | bytes 786436
  378.7 9.3 %copy-start.6 = (bf16[2,128,128]{2,1,0:T(8,128)(2,1)S(1)}, bf16[2,128,128]{2,1,0:T(8,128)(2,1)}, u32[]{:S(2)}) copy-start(bf16[2,128,128]{2,1,0:T(8,128)(2,1)} %copy-done.4) | copy-start | bytes 196612
  378.7 9.3 %copy-start.21 = (f32[4,256,128]{1,2,0:T(8,128)S(1)}, f32[4,256,128]{1,2,0:T(8,128)}, u32[]{:S(2)}) copy-start(f32[4,256,128]{1,2,0:T(8,128)} %convolution_add_fusion.9) | copy-start | bytes 1572868
  378.7 54.1 %all-to-all-start.7 = ((f32[16,128,256]{2,1,0:T(8,128)}), f32[16,128,256]{2,1,0:T(8,128)S(1)}, u32[]{:S(2)}, u32[]{:S(2)}) async-start(f32[16,128,256]{2,1,0:T(8,128)} %pad_maximum_fusion), calls=%async_computation.7 | async-start | bytes 4194304 | tf_op jit(solution)/shard_map/all_to_all | solution.py:124
  383.8 6.3 %copy-start.8 = (bf16[2,128,128]{2,1,0:T(8,128)(2,1)S(1)}, bf16[2,128,128]{2,1,0:T(8,128)(2,1)}, u32[]{:S(2)}) copy-start(bf16[2,128,128]{2,1,0:T(8,128)(2,1)} %get-tuple-element.68) | copy-start | bytes 196612
  383.9 6.3 %copy-start.23 = (bf16[4,256,256]{1,2,0:T(8,128)(2,1)S(1)}, bf16[4,256,256]{1,2,0:T(8,128)(2,1)}, u32[]{:S(2)}) copy-start(bf16[4,256,256]{1,2,0:T(8,128)(2,1)} %fusion.99) | copy-start | bytes 1572868
  384.6 5.8 %copy-start.11 = (bf16[4,256,256]{1,2,0:T(8,128)(2,1)S(1)}, bf16[4,256,256]{1,2,0:T(8,128)(2,1)}, u32[]{:S(2)}) copy-start(bf16[4,256,256]{1,2,0:T(8,128)(2,1)} %copy-done.10) | copy-start | bytes 1572868
  432.8 54.0 %all-to-all-start.6 = ((bf16[16,128,512]{2,1,0:T(8,128)(2,1)}), bf16[16,128,512]{2,1,0:T(8,128)(2,1)}, u32[]{:S(2)}, u32[]{:S(2)}) async-start(bf16[16,128,512]{2,1,0:T(8,128)(2,1)} %bitcast.705), calls=%async_computation.6 | async-start | bytes 4194304 | tf_op jit(solution)/shard_map/all_to_all | solution.py:122
  (201 other events, 539.6 us)
where the time goes:
time: 500 us; the launch traced here: 493 us
  waiting for transfers between devices  241 us (48%)
  matrix products  129 us (26%)
  local copies, waits for them, and re-layouts  58.9 us (12%)
  starting transfers between devices  41.8 us (8%)
  other arithmetic  18.5 us (4%)
    all_to_all x1, waiting for transfers between devices, per_device(): lax.all_to_all(outputs, 'seq', split_axis=1, concat_axis=0, tiled=True)  45.9 us
    all_to_all x1, waiting for transfers between devices, per_device(): lax.all_to_all(queries, 'seq', split_axis=1, concat_axis=0, tiled=True)  45.1 us
    all_to_all x1, waiting for transfers between devices, per_device(): lax.all_to_all(query_full, 'seq', split_axis=0, concat_axis=1, tiled=True)  40.2 us
    all_to_all x1, waiting for transfers between devices, per_device(): lax.all_to_all(out_grads, 'seq', split_axis=1, concat_axis=0, tiled=True)  38.3 us
    dot_general x21, matrix products, tile_scores(): jnp.einsum('qhd,kd->hqk', query_tile, key_tile, preferred_element_type=jn...  36.8 us
    all_to_all x1, waiting for transfers between devices, per_device(): lax.all_to_all(partials, 'seq', split_axis=0, concat_axis=1, tiled=True)  32.3 us
    dot_general x21, matrix products, tile_grads(): jnp.einsum('hqk,qhd->kd', score_low, query_tile, preferred_element_type=j...  28 us
    dot_general x21, matrix products, tile_grads(): jnp.einsum('qhd,kd->hqk', grad_tile, value_tile, preferred_element_type=j...  26.4 us
  transfers between devices with their start and end apart: 8, of which 8 were waited for; matrix products, arithmetic and copies ran while one was open for 9% of the time, Pallas kernels for 0%

commit v1 on v0

v1 whole, which is shorter than its diff:
```python
import functools
import math

import jax
import jax.numpy as jnp
from jax import lax
from jax.experimental import pallas as pl
from jax.experimental.pallas import tpu as pltpu
from jax.sharding import PartitionSpec as P

HEADS = 64
KVH = 8
HD = 128
GQA = HEADS // KVH
GW = GQA * HD
SCALE = HD ** (-0.5)
LOG2E = math.log2(math.e)
NT = (((1,), (1,)), ((), ()))
f32 = jnp.float32
bf16 = jnp.bfloat16

NEAR_AHEAD = 3


def kernel(
    starts, weights, q_hbm, do_hbm, o_hbm, k_ref, v_ref, ln_ref,
    dq_hbm, dk_ref, dv_ref,
    kv, q_s, do_s, o_s, bias, wcol, norm_t, p_s, ds_s, dq_s,
    pe_out, pe_in, own, a4_out, a4_in, f_out, f_in,
    in_sem, dq_sem, near_sem, far_sem, e1_sem, e3_sem, x1_sem, x3_sem, a4_sem, f_sem,
):
    tok = k_ref.shape[0]
    docs = starts.shape[0]
    me = lax.axis_index("seq")
    n = lax.axis_size("seq")
    up = {"seq": lax.rem(me + 2, n)}
    down = {"seq": lax.rem(me + n - 2, n)}
    parity = lax.rem(me, 2)
    mate = {"seq": me + 1 - 2 * parity}
    even = parity == 0

    def load(g, i):
        src = (q_hbm, do_hbm, o_hbm)[i]
        dst = (q_s, do_s, o_s)[i]
        return pltpu.make_async_copy(
            src.at[:, pl.ds(pl.multiple_of(g * GW, GW), GW)], dst.at[g], in_sem.at[i, g]
        )

    def dq_out(g):
        return pltpu.make_async_copy(
            dq_s.at[g], dq_hbm.at[:, pl.ds(pl.multiple_of(g * GW, GW), GW)], dq_sem.at[g]
        )

    def remote(src, dst, sem, g, where):
        return pltpu.make_async_remote_copy(
            src_ref=src, dst_ref=dst, send_sem=sem.at[0, g], recv_sem=sem.at[1, g],
            device_id=where, device_id_type=pl.DeviceIdType.MESH,
        )

    def rows(g, start):
        return kv.at[g, pl.ds(start, tok), :]

    def near(g):
        return remote(rows(g, 4 * tok), rows(g, 2 * tok), near_sem, g, up)

    def far(g):
        return remote(rows(g, 2 * tok), rows(g, 0), far_sem, g, up)

    def mate1(g):
        src = pl.multiple_of((4 - 2 * parity) * tok, tok)
        return remote(rows(g, src), rows(g, 3 * tok), e1_sem, g, mate)

    def mate3(g):
        src = pl.multiple_of((2 - 2 * parity) * tok, tok)
        return remote(rows(g, src), rows(g, tok), e3_sem, g, mate)

    def back1(g):
        return remote(pe_out.at[g, 1], pe_in.at[g, 1], x1_sem, g, mate)

    def back3(g):
        return remote(pe_out.at[g, 0], pe_in.at[g, 0], x3_sem, g, mate)

    def back_far(g):
        return remote(a4_out.at[g], a4_in.at[g], a4_sem, g, down)

    def back_near(g):
        return remote(f_out.at[g], f_in.at[g], f_sem, g, down)

    def each(lo, hi, fn):
        def step(i, carry):
            fn(i)
            return carry
        lax.fori_loop(lo, hi, step, 0)

    for i in range(3):
        each(0, KVH, lambda g: load(g, i).start())

    barrier = pltpu.get_barrier_semaphore()
    for where in (up, down, mate):
        pl.semaphore_signal(barrier, inc=1, device_id=where, device_id_type=pl.DeviceIdType.MESH)
    for g in range(KVH):
        kv[g, 4 * tok :, 0:HD] = k_ref[:, g * HD : (g + 1) * HD]
        kv[g, 4 * tok :, HD:] = v_ref[:, g * HD : (g + 1) * HD]
    pl.semaphore_wait(barrier, 3)

    for g in range(NEAR_AHEAD):
        near(g).start()

    base = me * tok
    pos_lane = lax.broadcasted_iota(jnp.int32, (8, tok), 1) + base
    pos_row = lax.broadcasted_iota(jnp.int32, (tok, HD), 0) + base
    start_row = jnp.zeros((8, tok), jnp.int32)
    w_row = jnp.zeros((8, tok), f32)
    w_col = jnp.zeros((tok, HD), f32)
    for d in range(docs):
        start_row = jnp.where(pos_lane >= starts[d], starts[d], start_row)
        w_row = jnp.where(pos_lane >= starts[d], weights[d], w_row)
        w_col = jnp.where(pos_row >= starts[d], weights[d], w_col)
    wcol[...] = w_col * (-SCALE)
    w_row = w_row[0:1] * SCALE
    key_pos = lax.broadcasted_iota(jnp.int32, (5 * tok, tok), 0) + (base - 4 * tok)
    query_pos = lax.broadcasted_iota(jnp.int32, (5 * tok, tok), 1) + base
    allowed = (key_pos >= start_row[0:1]) & (key_pos <= query_pos)
    bias[...] = jnp.where(allowed, 0.0, -1e30).astype(f32)
    norm_t[...] = ln_ref[...].T * LOG2E
    lane = lax.broadcasted_iota(jnp.int32, (tok, HD), 1)

    def arrive_near(g):
        near(g).wait_recv()
        far(g).start()
        mate1(g).start()

    def arrive_far(g):
        far(g).wait_recv()
        mate3(g).start()

    def arrive_mate(g):
        mate1(g).wait_recv()
        mate3(g).wait_recv()

    def compute(g):
        kvw = kv[g]
        delta = jnp.zeros((tok, HD), f32)
        for h in range(GQA):
            cols = slice(h * HD, (h + 1) * HD)
            prod = do_s[g, :, cols].astype(f32) * o_s[g, :, cols].astype(f32)
            delta = jnp.where(lane == h, jnp.sum(prod, axis=1, keepdims=True), delta)
        delta = delta.T[0:GQA]
        norm = norm_t[pl.ds(pl.multiple_of(g * GQA, GQA), GQA), :]
        mask = bias[...]
        for h in range(GQA):
            cols = slice(h * HD, (h + 1) * HD)
            q = q_s[g, :, cols]
            do = do_s[g, :, cols]
            wq = (q.astype(f32) * wcol[...]).astype(bf16)
            s = lax.dot_general(kvw[:, :HD], q, NT, preferred_element_type=f32)
            gs = lax.dot_general(
                kvw, jnp.concatenate([wq, do], 1), NT, preferred_element_type=f32
            )
            p = jnp.exp2(s * (SCALE * LOG2E) + mask - norm[h : h + 1])
            mean = jnp.sum(p * s, axis=0, keepdims=True)
            ds = p * (gs + (w_row * mean - delta[h : h + 1]))
            p_s[:, cols] = p.astype(bf16)
            ds_s[:, cols] = ds.astype(bf16)
        q_all = jnp.concatenate([q_s[g, :, h * HD : (h + 1) * HD] for h in range(GQA)], 0)
        do_all = jnp.concatenate([do_s[g, :, h * HD : (h + 1) * HD] for h in range(GQA)], 0)
        dk = jnp.dot(ds_s[...], q_all, preferred_element_type=f32) * SCALE
        dv = jnp.dot(p_s[...], do_all, preferred_element_type=f32)
        for part, block in enumerate((dk, dv)):
            cols = slice(part * HD, (part + 1) * HD)
            own[g, 2, :, cols] = block[0:tok]
            pe_out[g, 0, :, cols] = block[tok : 2 * tok].astype(bf16)
            own[g, 1, :, cols] = block[2 * tok : 3 * tok]
            pe_out[g, 1, :, cols] = block[3 * tok : 4 * tok].astype(bf16)
            own[g, 0, :, cols] = block[4 * tok :]
        back1(g).start()
        back3(g).start()
        dq_t = jnp.dot(kvw[:, :HD].T, ds_s[...], preferred_element_type=f32) * SCALE
        for h in range(GQA):
            cols = slice(h * HD, (h + 1) * HD)
            dq_s[g, :, cols] = dq_t[:, cols].T.astype(bf16)
        dq_out(g).start()

    def grads_mate(g):
        back1(g).wait_recv()
        back3(g).wait_recv()
        one = pe_in[g, 1].astype(f32)
        three = pe_in[g, 0].astype(f32)
        zero = jnp.zeros_like(one)
        a4_out[g] = (own[g, 2] + jnp.where(even, zero, three)).astype(bf16)
        back_far(g).start()
        own[g, 1] = own[g, 1] + jnp.where(even, three, one)
        own[g, 0] = own[g, 0] + jnp.where(even, one, zero)

    def grads_far(g):
        back_far(g).wait_recv()
        f_out[g] = (own[g, 1] + a4_in[g].astype(f32)).astype(bf16)
        back_near(g).start()

    def grads_near(g):
        back_near(g).wait_recv()
        total = (own[g, 0] + f_in[g].astype(f32)).astype(bf16)
        cols = pl.ds(pl.multiple_of(g * HD, HD), HD)
        dk_ref[:, cols] = total[:, :HD]
        dv_ref[:, cols] = total[:, HD:]

    arrive_near(0)
    near(NEAR_AHEAD).start()
    arrive_near(1)
    near(NEAR_AHEAD + 1).start()
    arrive_far(0)

    def step(g, carry):
        @pl.when(g + 2 < KVH)
        def _():
            arrive_near(g + 2)

        @pl.when(g + 2 + NEAR_AHEAD < KVH)
        def _():
            near(g + 2 + NEAR_AHEAD).start()

        @pl.when(g + 1 < KVH)
        def _():
            arrive_far(g + 1)

        arrive_mate(g)
        for i in range(3):
            load(g, i).wait()
        compute(g)

        @pl.when(g >= 1)
        def _():
            grads_mate(g - 1)

        @pl.when(g >= 2)
        def _():
            grads_far(g - 2)

        @pl.when(g >= 3)
        def _():
            grads_near(g - 3)

        return carry

    lax.fori_loop(0, KVH, step, 0)
    grads_mate(KVH - 1)
    grads_far(KVH - 2)
    grads_near(KVH - 3)
    grads_far(KVH - 1)
    grads_near(KVH - 2)
    grads_near(KVH - 1)

    def finish(g, carry):
        for copy in (near, far, mate1, mate3, back1, back3, back_far, back_near):
            copy(g).wait_send()
        dq_out(g).wait()
        return carry

    lax.fori_loop(0, KVH, finish, 0)


def per_device(
    queries, key_rows, value_rows, outputs, out_grads, log_normalizer, doc_starts, doc_weights
):
    tok = queries.shape[0]
    vmem = pl.BlockSpec(memory_space=pltpu.VMEM)
    smem = pl.BlockSpec(memory_space=pltpu.SMEM)
    hbm = pl.BlockSpec(memory_space=pl.ANY)
    dma = pltpu.SemaphoreType.DMA
    block = (KVH, tok, 2 * HD)
    return pl.pallas_call(
        kernel,
        out_shape=(
            jax.ShapeDtypeStruct(queries.shape, bf16),
            jax.ShapeDtypeStruct(key_rows.shape, bf16),
            jax.ShapeDtypeStruct(value_rows.shape, bf16),
        ),
        in_specs=[smem, smem, hbm, hbm, hbm, vmem, vmem, vmem],
        out_specs=(hbm, vmem, vmem),
        scratch_shapes=[
            pltpu.VMEM((KVH, 5 * tok, 2 * HD), bf16),
            pltpu.VMEM((KVH, tok, GW), bf16),
            pltpu.VMEM((KVH, tok, GW), bf16),
            pltpu.VMEM((KVH, tok, GW), bf16),
            pltpu.VMEM((5 * tok, tok), f32),
            pltpu.VMEM((tok, HD), f32),
            pltpu.VMEM((HEADS, tok), f32),
            pltpu.VMEM((5 * tok, GW), bf16),
            pltpu.VMEM((5 * tok, GW), bf16),
            pltpu.VMEM((KVH, tok, GW), bf16),
            pltpu.VMEM((KVH, 2, tok, 2 * HD), bf16),
            pltpu.VMEM((KVH, 2, tok, 2 * HD), bf16),
            pltpu.VMEM((KVH, 3, tok, 2 * HD), f32),
            pltpu.VMEM(block, bf16),
            pltpu.VMEM(block, bf16),
            pltpu.VMEM(block, bf16),
            pltpu.VMEM(block, bf16),
            dma((3, KVH)),
            dma((KVH,)),
        ]
        + [dma((2, KVH))] * 8,
        compiler_params=pltpu.CompilerParams(
            collective_id=0, has_side_effects=True, vmem_limit_bytes=56 * 1024 * 1024
        ),
        cost_estimate=pl.CostEstimate(
            flops=10 * HEADS * tok * 5 * tok * HD, bytes_accessed=9 * queries.size, transcendentals=0
        ),
    )(doc_starts, doc_weights, queries, out_grads, outputs, key_rows, value_rows, log_normalizer)


def solution(mesh):
    rows = P(("dp", "seq"), None)
    in_specs = (rows, rows, rows, rows, rows, rows, P("dp"), P("dp"))
    return jax.shard_map(
        per_device, mesh=mesh, in_specs=in_specs, out_specs=(rows, rows, rows), check_vma=False
    )
```

time: 500 us -> 65.7 us (0.13)
  the two profiles are of different devices: /device:TPU:1 before, /device:TPU:36 now
where the time goes in v1:
time: 65.7 us; the launch traced here: 65.5 us
  Pallas kernels  58.8 us (89%)
  local copies, waits for them, and re-layouts  6.05 us (9%)
  between operations  0.66 us (1%)
    pallas_call x1, Pallas kernels, per_device(): pl.pallas_call(kernel, out_shape=(jax.ShapeDtypeStruct(queries.shape, bf1...  58.8 us
    unnamed x8, local copies, waits for them, and re-layouts  6.05 us

profile of v1, /device:TPU:36, one launch (start us, length us, event | category | flops | bytes accessed | tf_op | source)
XLA Modules:
  0.0 65.5 jit_solution(11100748082198273188)
XLA Ops:
  0.6 1.5 %copy.11.ln_ref = f32[128,64]{1,0:T(8,128)} copy(f32[128,64]{0,1:T(8,128)} %param.13) | data formatting | bytes 65536 | tf_op args[5]
  2.1 58.8 %shard_map.103 = (bf16[128,8192]{1,0:T(8,128)(2,1)}, bf16[128,1024]{1,0:T(8,128)(2,1)}, bf16[128,1024]{1,0:T(8,128)(2,1)}) custom-call(s32[8]{0:T(128)} %starts.1, f32[8]{0:T(128)} %weights.1, bf16[128,8192]{1,0:T(8,128)(2,1)} %q_hbm.1, bf16[128,8192]{1,0:T(8,128)(2,1)} %do_hbm.1, bf16[128,8192]{1,0:T(8,128)(2,1)} %o_hbm.1, bf16[128,1024]{1,0:T(8,128)(2,1)} %k_ref.1, ...), custom_call_target="tpu_custom_call" | custom-call | flops 6710886400 | bytes 9437184 | tf_op jit(solution)/shard_map/pallas_call | solution.py:271
  60.9 0.0 copy-start.1
  60.9 0.0 copy-start
  60.9 3.2 %copy.15 = bf16[128,8192]{1,0:T(8,128)(2,1)} copy(bf16[128,8192]{1,0:T(8,128)(2,1)} %get-tuple-element.6) | data formatting | bytes 4194304
  64.1 0.0 copy-done.1
  64.1 0.7 %copy.16 = bf16[128,1024]{1,0:T(8,128)(2,1)} copy(bf16[128,1024]{1,0:T(8,128)(2,1)S(1)} %copy-done.1) | data formatting | bytes 524288
  64.8 0.0 copy-done
  64.8 0.7 %copy.17 = bf16[128,1024]{1,0:T(8,128)(2,1)} copy(bf16[128,1024]{1,0:T(8,128)(2,1)S(1)} %copy-done) | data formatting | bytes 524288
Async XLA Ops:
  60.9 3.2 %copy-start.1 = (bf16[128,1024]{1,0:T(8,128)(2,1)S(1)}, bf16[128,1024]{1,0:T(8,128)(2,1)}, u32[]{:S(2)}) copy-start(bf16[128,1024]{1,0:T(8,128)(2,1)} %get-tuple-element.7) | copy-start | bytes 786436
  60.9 3.9 %copy-start = (bf16[128,1024]{1,0:T(8,128)(2,1)S(1)}, bf16[128,1024]{1,0:T(8,128)(2,1)}, u32[]{:S(2)}) copy-start(bf16[128,1024]{1,0:T(8,128)(2,1)} %get-tuple-element.8) | copy-start | bytes 786436

commit v2 on v1

v2 whole, which is shorter than its diff:
```python
import functools
import math

import jax
import jax.numpy as jnp
from jax import lax
from jax.experimental import pallas as pl
from jax.experimental.pallas import tpu as pltpu
from jax.sharding import PartitionSpec as P

HEADS = 64
KVH = 8
HD = 128
GQA = HEADS // KVH
GW = GQA * HD
SCALE = HD ** (-0.5)
LOG2E = math.log2(math.e)
NT = (((1,), (1,)), ((), ()))
VMEM_BYTES = 56 * 1024 * 1024
f32 = jnp.float32
bf16 = jnp.bfloat16

AHEAD_SEND = 7
AHEAD_PASS = 4
AHEAD_PAIR = 2
LAG_PASS = 4
LAG_LAST = 7
STRAIGHT = 2


def kernel(
    starts, weights, q_hbm, do_hbm, o_hbm, k_hbm, v_hbm, norm_hbm,
    dq_ref, dk_ref, dv_ref,
    kv, q_s, do_s, o_s, bias, wcol, norm_t, delta_t, mean_t, p32_s, p_s, ds_s, k_s, v_s, norm_s,
    pair_out, pair_in, own, far_out, far_in, near_out, near_in,
    in_sem, small_sem, near_sem, far_sem, mate_sem, pair_sem, back_far_sem, back_near_sem,
):
    tok = k_hbm.shape[0]
    docs = starts.shape[0]
    units = 2 * KVH
    me = lax.axis_index("seq")
    n = lax.axis_size("seq")
    parity = lax.rem(me, 2)
    even = parity == 0
    up = {"seq": lax.rem(me + 2, n)}
    up_two = {"seq": lax.rem(me + 4, n)}
    down = {"seq": lax.rem(me + n - 2, n)}
    down_two = {"seq": lax.rem(me + n - 4, n)}
    mate = {"seq": me + 1 - 2 * parity}

    def load(g, i):
        src = (q_hbm, do_hbm, o_hbm)[i]
        dst = (q_s, do_s, o_s)[i]
        return pltpu.make_async_copy(
            src.at[:, pl.ds(pl.multiple_of(g * GW, GW), GW)], dst.at[g], in_sem.at[i, g]
        )

    def load_small(i):
        src = (k_hbm, v_hbm, norm_hbm)[i]
        dst = (k_s, v_s, norm_s)[i]
        return pltpu.make_async_copy(src, dst, small_sem.at[i])

    def remote(src, dst, sem, u, where):
        return pltpu.make_async_remote_copy(
            src_ref=src, dst_ref=dst, send_sem=sem.at[0, u], recv_sem=sem.at[1, u],
            device_id=where, device_id_type=pl.DeviceIdType.MESH,
        )

    def rows(u, start, size=1):
        return kv.at[u, pl.ds(start, size * tok), :]

    def near(u):
        return remote(rows(u, 0), rows(u, tok), near_sem, u, up)

    def far(u):
        return remote(rows(u, tok), rows(u, 2 * tok), far_sem, u, up)

    def share(u):
        src = pl.multiple_of(parity * tok, tok)
        return remote(rows(u, src, 2), rows(u, 3 * tok, 2), mate_sem, u, mate)

    def pair(u):
        return remote(pair_out.at[u], pair_in.at[u], pair_sem, u, mate)

    def back_far(u):
        return remote(far_out.at[u], far_in.at[u], back_far_sem, u, down)

    def back_far_two(u):
        return remote(far_out.at[u], far_in.at[u], back_far_sem, u, down_two)

    def back_near(u):
        return remote(near_out.at[u], near_in.at[u], back_near_sem, u, down)

    def each(lo, hi, fn):
        def step(i, carry):
            fn(i)
            return carry
        lax.fori_loop(lo, hi, step, 0)

    barrier = pltpu.get_barrier_semaphore()
    partners = (up, down, mate, up_two, down_two)
    for where in partners:
        pl.semaphore_signal(barrier, inc=1, device_id=where, device_id_type=pl.DeviceIdType.MESH)
    for i in range(3):
        load_small(i).start()
    for i in (1, 2, 0):
        each(0, KVH, lambda g: load(g, i).start())
    load_small(0).wait()
    load_small(1).wait()
    for g in range(KVH):
        kv[2 * g, 0:tok, :] = k_s[:, g * HD : (g + 1) * HD]
        kv[2 * g + 1, 0:tok, :] = v_s[:, g * HD : (g + 1) * HD]
    pl.semaphore_wait(barrier, len(partners))
    for u in range(AHEAD_PASS):
        near(u).start()

    base = me * tok
    pos_lane = lax.broadcasted_iota(jnp.int32, (8, tok), 1) + base
    pos_row = lax.broadcasted_iota(jnp.int32, (tok, HD), 0) + base
    start_row = jnp.zeros((8, tok), jnp.int32)
    w_row = jnp.zeros((8, tok), f32)
    w_col = jnp.zeros((tok, HD), f32)
    for d in range(docs):
        start_row = jnp.where(pos_lane >= starts[d], starts[d], start_row)
        w_row = jnp.where(pos_lane >= starts[d], weights[d], w_row)
        w_col = jnp.where(pos_row >= starts[d], weights[d], w_col)
    wcol[...] = w_col * (-SCALE)
    w_row = w_row[0:1] * SCALE
    query_pos = lax.broadcasted_iota(jnp.int32, (tok, tok), 1) + base
    for i, behind in enumerate((0, 2, 4, 1, 3)):
        key_pos = lax.broadcasted_iota(jnp.int32, (tok, tok), 0) + (base - behind * tok)
        allowed = (key_pos >= start_row[0:1]) & (key_pos <= query_pos)
        bias[i * tok : (i + 1) * tok, :] = jnp.where(allowed, 0.0, -1e30).astype(f32)
    load_small(2).wait()
    norm_t[...] = norm_s[...] * LOG2E
    lane = lax.broadcasted_iota(jnp.int32, (tok, HD), 1)

    def row_deltas(g):
        load(g, 1).wait()
        load(g, 2).wait()
        delta = jnp.zeros((tok, HD), f32)
        for h in range(GQA):
            cols = slice(h * HD, (h + 1) * HD)
            prod = do_s[g, :, cols].astype(f32) * o_s[g, :, cols].astype(f32)
            delta = jnp.where(lane == h, jnp.sum(prod, axis=1, keepdims=True), delta)
        delta_t[pl.ds(pl.multiple_of(g * GQA, GQA), GQA), :] = delta.T[0:GQA]

    each(0, KVH, row_deltas)
    each(0, KVH, lambda g: load(g, 0).wait())

    def pass_on(u):
        near(u).wait_recv()
        far(u).start()

    def give_mate(u):
        far(u).wait_recv()
        share(u).start()

    def put_grad(u, block):
        pair_out[u] = block[3 * tok :].astype(bf16)
        pair(u).start()
        own[u] = block[0 : 3 * tok]

    def stack(ref, g):
        return jnp.concatenate([ref[g, :, h * HD : (h + 1) * HD] for h in range(GQA)], 0)

    def probs_phase(g):
        keys = kv[2 * g]
        norm = norm_t[pl.ds(pl.multiple_of(g * GQA, GQA), GQA), :]
        mask = bias[...]
        for h in range(GQA):
            cols = slice(h * HD, (h + 1) * HD)
            s = lax.dot_general(keys, q_s[g, :, cols], NT, preferred_element_type=f32)
            p = jnp.exp2(s * (SCALE * LOG2E) + mask - norm[h : h + 1])
            mean_t[h : h + 1, :] = jnp.sum(p * s, axis=0, keepdims=True)
            p32_s[:, cols] = p
            p_s[:, cols] = p.astype(bf16)
        put_grad(2 * g, jnp.dot(p_s[...], stack(do_s, g), preferred_element_type=f32))

    def grads_phase(g):
        window = jnp.concatenate([kv[2 * g], kv[2 * g + 1]], 1)
        delta = delta_t[pl.ds(pl.multiple_of(g * GQA, GQA), GQA), :]
        offset = w_row * mean_t[...] - delta
        for h in range(GQA):
            cols = slice(h * HD, (h + 1) * HD)
            wq = (q_s[g, :, cols].astype(f32) * wcol[...]).astype(bf16)
            gs = lax.dot_general(
                window, jnp.concatenate([wq, do_s[g, :, cols]], 1), NT, preferred_element_type=f32
            )
            ds_s[g, :, cols] = (p32_s[:, cols] * (gs + offset[h : h + 1])).astype(bf16)
        put_grad(
            2 * g + 1, jnp.dot(ds_s[g], stack(q_s, g), preferred_element_type=f32) * SCALE
        )

    def query_phase(g):
        dq_t = jnp.dot(kv[2 * g].T, ds_s[g], preferred_element_type=f32) * SCALE
        for h in range(GQA):
            cols = slice(h * HD, (h + 1) * HD)
            dq_ref[g, :, cols] = dq_t[:, cols].T.astype(bf16)

    def grads_mate(u):
        pair(u).wait_recv()
        one = pair_in[u, 0:tok].astype(f32)
        three = pair_in[u, tok:].astype(f32)
        zero = jnp.zeros_like(one)
        far_out[u] = (own[u, 2 * tok :] + jnp.where(even, zero, three)).astype(bf16)
        own[u, 0:tok] = own[u, 0:tok] + jnp.where(even, one, zero)
        return own[u, tok : 2 * tok] + jnp.where(even, three, one)

    def grads_mate_pass(u):
        block = grads_mate(u)
        back_far(u).start()
        own[u, tok : 2 * tok] = block

    def grads_mate_straight(u):
        near_out[u] = grads_mate(u).astype(bf16)
        back_near(u).start()
        back_far_two(u).start()

    def grads_pass(u):
        back_far(u).wait_recv()
        near_out[u] = (own[u, tok : 2 * tok] + far_in[u].astype(f32)).astype(bf16)
        back_near(u).start()

    def grads_last(u):
        back_near(u).wait_recv()
        own[u, 0:tok] = own[u, 0:tok] + near_in[u].astype(f32)

    def grads_last_straight(u):
        back_far_two(u).wait_recv()
        own[u, 0:tok] = own[u, 0:tok] + far_in[u].astype(f32)
        grads_last(u)

    def between(u):
        @pl.when(u + AHEAD_PASS < units)
        def _():
            pass_on(u + AHEAD_PASS)

        @pl.when(u + AHEAD_SEND < units)
        def _():
            near(u + AHEAD_SEND).start()

        @pl.when(u + AHEAD_PAIR < units)
        def _():
            give_mate(u + AHEAD_PAIR)

        @pl.when((u >= 1) & (u - 1 < units - STRAIGHT))
        def _():
            grads_mate_pass(u - 1)

        @pl.when(u - 1 >= units - STRAIGHT)
        def _():
            grads_mate_straight(u - 1)

        @pl.when(u >= LAG_PASS)
        def _():
            grads_pass(u - LAG_PASS)

        @pl.when(u >= LAG_LAST)
        def _():
            grads_last(u - LAG_LAST)

    for u in range(AHEAD_PASS):
        pass_on(u)
        if AHEAD_PASS + u < AHEAD_SEND:
            near(AHEAD_PASS + u).start()
    for u in range(2 * AHEAD_PASS, AHEAD_SEND):
        near(u).start()
    for u in range(AHEAD_PAIR):
        give_mate(u)

    def step(g, carry):
        share(2 * g).wait_recv()
        probs_phase(g)
        between(2 * g)
        share(2 * g + 1).wait_recv()
        grads_phase(g)
        between(2 * g + 1)
        return carry

    lax.fori_loop(0, KVH, step, 0)
    grads_mate_straight(units - 1)
    each(units - LAG_PASS, units - STRAIGHT, grads_pass)
    each(0, KVH, query_phase)
    each(units - LAG_LAST, units - STRAIGHT, grads_last)
    each(units - STRAIGHT, units, grads_last_straight)
    for g in range(KVH):
        cols = slice(g * HD, (g + 1) * HD)
        dv_ref[:, cols] = own[2 * g, 0:tok].astype(bf16)
        dk_ref[:, cols] = own[2 * g + 1, 0:tok].astype(bf16)

    def finish(u):
        for copy in (near, far, share, pair, back_far, back_near):
            copy(u).wait_send()

    each(0, units, finish)


def out_kernel(dq_in, dk_in, dv_in, dq, dk, dv, sems):
    groups = dq_in.shape[0]
    copies = [
        pltpu.make_async_copy(dq_in.at[g], dq.at[:, g * GW : (g + 1) * GW], sems.at[g])
        for g in range(groups)
    ]
    copies.append(pltpu.make_async_copy(dk_in, dk, sems.at[groups]))
    copies.append(pltpu.make_async_copy(dv_in, dv, sems.at[groups + 1]))
    for copy in copies:
        copy.start()
    for copy in copies:
        copy.wait()


def finish_out(dq, dk, dv):
    vmem = pl.BlockSpec(memory_space=pltpu.VMEM)
    hbm = pl.BlockSpec(memory_space=pl.ANY)
    groups, tok, width = dq.shape
    return pl.pallas_call(
        out_kernel,
        out_shape=(
            jax.ShapeDtypeStruct((tok, groups * width), dq.dtype),
            jax.ShapeDtypeStruct(dk.shape, dk.dtype),
            jax.ShapeDtypeStruct(dv.shape, dv.dtype),
        ),
        in_specs=[vmem] * 3,
        out_specs=(hbm,) * 3,
        scratch_shapes=[pltpu.SemaphoreType.DMA((groups + 2,))],
        compiler_params=pltpu.CompilerParams(vmem_limit_bytes=VMEM_BYTES),
    )(dq, dk, dv)


def per_device(
    queries, key_rows, value_rows, outputs, out_grads, log_normalizer, doc_starts, doc_weights
):
    tok = queries.shape[0]
    units = 2 * KVH
    vmem = pl.BlockSpec(memory_space=pltpu.VMEM)
    smem = pl.BlockSpec(memory_space=pltpu.SMEM)
    hbm = pl.BlockSpec(memory_space=pl.ANY)
    dma = pltpu.SemaphoreType.DMA
    heads = pltpu.VMEM((KVH, tok, GW), bf16)
    block = pltpu.VMEM((units, tok, HD), bf16)
    pair = pltpu.VMEM((units, 2 * tok, HD), bf16)
    tile = pltpu.VMEM((5 * tok, GW), bf16)
    out = pl.pallas_call(
        kernel,
        out_shape=(
            pltpu.VMEM((KVH, tok, GW), bf16),
            pltpu.VMEM(key_rows.shape, bf16),
            pltpu.VMEM(value_rows.shape, bf16),
        ),
        in_specs=[smem, smem] + [hbm] * 6,
        out_specs=(vmem,) * 3,
        scratch_shapes=[
            pltpu.VMEM((units, 5 * tok, HD), bf16),
            heads, heads, heads,
            pltpu.VMEM((5 * tok, tok), f32),
            pltpu.VMEM((tok, HD), f32),
            pltpu.VMEM((HEADS, tok), f32),
            pltpu.VMEM((HEADS, tok), f32),
            pltpu.VMEM((GQA, tok), f32),
            pltpu.VMEM((5 * tok, GW), f32),
            tile,
            pltpu.VMEM((KVH, 5 * tok, GW), bf16),
            pltpu.VMEM(key_rows.shape, bf16),
            pltpu.VMEM(value_rows.shape, bf16),
            pltpu.VMEM((HEADS, tok), f32),
            pair, pair,
            pltpu.VMEM((units, 3 * tok, HD), f32),
            block, block, block, block,
            dma((3, KVH)),
            dma((3,)),
        ]
        + [dma((2, units))] * 6,
        compiler_params=pltpu.CompilerParams(
            collective_id=0, has_side_effects=True, vmem_limit_bytes=VMEM_BYTES
        ),
        cost_estimate=pl.CostEstimate(
            flops=10 * HEADS * tok * 5 * tok * HD, bytes_accessed=9 * queries.size, transcendentals=0
        ),
    )(doc_starts, doc_weights, queries, out_grads, outputs, key_rows, value_rows, log_normalizer.T)
    return finish_out(*[pltpu.with_memory_space_constraint(x, pltpu.VMEM) for x in out])


def solution(mesh):
    rows = P(("dp", "seq"), None)
    in_specs = (rows, rows, rows, rows, rows, rows, P("dp"), P("dp"))
    return jax.shard_map(
        per_device, mesh=mesh, in_specs=in_specs, out_specs=(rows, rows, rows), check_vma=False
    )
```

time: 65.7 us -> 52.3 us (0.80)
  the two profiles are of different devices: /device:TPU:36 before, /device:TPU:1 now
where the time goes in v2:
time: 52.3 us
  Pallas kernels  51.6 us (99%)
  between operations  0.64 us (1%)
    pallas_call x1, Pallas kernels, per_device(): pl.pallas_call(kernel, out_shape=(pltpu.VMEM((KVH, tok, GW), bf16), pltpu...  50 us
    pallas_call x1, Pallas kernels, finish_out(): pl.pallas_call(out_kernel, out_shape=(jax.ShapeDtypeStruct((tok, groups *...  1.57 us

profile of v2, /device:TPU:1, one launch (start us, length us, event | category | flops | bytes accessed | tf_op | source)
XLA Modules:
  0.0 52.3 jit_solution(7699914795681300254)
XLA Ops:
  0.6 50.0 %shard_map.103 = (bf16[8,128,1024]{2,1,0:T(8,128)(2,1)S(1)}, bf16[128,1024]{1,0:T(8,128)(2,1)S(1)}, bf16[128,1024]{1,0:T(8,128)(2,1)S(1)}) custom-call(s32[8]{0:T(128)} %starts.1, f32[8]{0:T(128)} %weights.1, bf16[128,8192]{1,0:T(8,128)(2,1)} %q_hbm.1, bf16[128,8192]{1,0:T(8,128)(2,1)} %do_hbm.1, bf16[128,8192]{1,0:T(8,128)(2,1)} %o_hbm.1, ...), custom_call_target="tpu_custom_call" | custom-call | flops 6710886400 | bytes 9437184 | tf_op jit(solution)/shard_map/pallas_call | solution.py:344
  50.7 1.6 %shard_map.104 = (bf16[128,8192]{1,0:T(8,128)(2,1)}, bf16[128,1024]{1,0:T(8,128)(2,1)}, bf16[128,1024]{1,0:T(8,128)(2,1)}) custom-call(bf16[8,128,1024]{2,1,0:T(8,128)(2,1)S(1)} %get-tuple-element.6.dq_in, bf16[128,1024]{1,0:T(8,128)(2,1)S(1)} %get-tuple-element.7.dk_in, bf16[128,1024]{1,0:T(8,128)(2,1)S(1)} %get-tuple-element.8.dv_in), custom_call_target="tpu_custom_call" | custom-call | tf_op jit(solution)/shard_map/pallas_call | solution.py:317

commit v3 on v2

--- a/solution.py
+++ b/solution.py
@@ -20,12 +20,13 @@
 f32 = jnp.float32
 bf16 = jnp.bfloat16
 
-AHEAD_SEND = 7
-AHEAD_PASS = 4
+AHEAD_SEND = 8
+AHEAD_PASS = 5
 AHEAD_PAIR = 2
 LAG_PASS = 4
 LAG_LAST = 7
-STRAIGHT = 2
+STRAIGHT_FIRST = 0
+STRAIGHT_LAST = 1
 
 
 def kernel(
@@ -170,7 +171,10 @@
         mask = bias[...]
         for h in range(GQA):
             cols = slice(h * HD, (h + 1) * HD)
-            s = lax.dot_general(keys, q_s[g, :, cols], NT, preferred_element_type=f32)
+            if h % 2 == 0:
+                two = jnp.concatenate([q_s[g, :, cols], q_s[g, :, (h + 1) * HD : (h + 2) * HD]], 0)
+                both = lax.dot_general(keys, two, NT, preferred_element_type=f32)
+            s = both[:, (h % 2) * HD : (h % 2 + 1) * HD]
             p = jnp.exp2(s * (SCALE * LOG2E) + mask - norm[h : h + 1])
             mean_t[h : h + 1, :] = jnp.sum(p * s, axis=0, keepdims=True)
             p32_s[:, cols] = p
@@ -183,10 +187,13 @@
         offset = w_row * mean_t[...] - delta
         for h in range(GQA):
             cols = slice(h * HD, (h + 1) * HD)
-            wq = (q_s[g, :, cols].astype(f32) * wcol[...]).astype(bf16)
-            gs = lax.dot_general(
-                window, jnp.concatenate([wq, do_s[g, :, cols]], 1), NT, preferred_element_type=f32
-            )
+            if h % 2 == 0:
+                sides = [
+                    jnp.concatenate([(q_s[g, :, c].astype(f32) * wcol[...]).astype(bf16), do_s[g, :, c]], 1)
+                    for c in (cols, slice((h + 1) * HD, (h + 2) * HD))
+                ]
+                both = lax.dot_general(window, jnp.concatenate(sides, 0), NT, preferred_element_type=f32)
+            gs = both[:, (h % 2) * HD : (h % 2 + 1) * HD]
             ds_s[g, :, cols] = (p32_s[:, cols] * (gs + offset[h : h + 1])).astype(bf16)
         put_grad(
             2 * g + 1, jnp.dot(ds_s[g], stack(q_s, g), preferred_element_type=f32) * SCALE
@@ -213,25 +220,42 @@
         own[u, tok : 2 * tok] = block
 
     def grads_mate_straight(u):
-        near_out[u] = grads_mate(u).astype(bf16)
+        block = grads_mate(u)
+        back_far_two(u).start()
+        near_out[u] = block.astype(bf16)
         back_near(u).start()
-        back_far_two(u).start()
 
     def grads_pass(u):
         back_far(u).wait_recv()
         near_out[u] = (own[u, tok : 2 * tok] + far_in[u].astype(f32)).astype(bf16)
         back_near(u).start()
 
-    def grads_last(u):
+    def last(u):
+        @pl.when((u < STRAIGHT_FIRST) | (u >= units - STRAIGHT_LAST))
+        def _():
+            back_far_two(u).wait_recv()
+            own[u, 0:tok] = own[u, 0:tok] + far_in[u].astype(f32)
+
         back_near(u).wait_recv()
-        own[u, 0:tok] = own[u, 0:tok] + near_in[u].astype(f32)
-
-    def grads_last_straight(u):
-        back_far_two(u).wait_recv()
-        own[u, 0:tok] = own[u, 0:tok] + far_in[u].astype(f32)
-        grads_last(u)
+        total = (own[u, 0:tok] + near_in[u].astype(f32)).astype(bf16)
+        cols = pl.ds(pl.multiple_of((u // 2) * HD, HD), HD)
+
+        @pl.when(u % 2 == 0)
+        def _():
+            dv_ref[:, cols] = total
+
+        @pl.when(u % 2 == 1)
+        def _():
+            dk_ref[:, cols] = total
+
+    def merge(u):
+        straight = ((u >= 0) & (u < STRAIGHT_FIRST)) | (u >= units - STRAIGHT_LAST)
+        pl.when(straight)(lambda: grads_mate_straight(u))
+        pl.when((u >= 0) & jnp.logical_not(straight))(lambda: grads_mate_pass(u))
 
     def between(u):
+        merge(u - 1)
+
         @pl.when(u + AHEAD_PASS < units)
         def _():
             pass_on(u + AHEAD_PASS)
@@ -244,21 +268,13 @@
         def _():
             give_mate(u + AHEAD_PAIR)
 
-        @pl.when((u >= 1) & (u - 1 < units - STRAIGHT))
-        def _():
-            grads_mate_pass(u - 1)
-
-        @pl.when(u - 1 >= units - STRAIGHT)
-        def _():
-            grads_mate_straight(u - 1)
-
-        @pl.when(u >= LAG_PASS)
+        @pl.when(u >= LAG_PASS + STRAIGHT_FIRST)
         def _():
             grads_pass(u - LAG_PASS)
 
         @pl.when(u >= LAG_LAST)
         def _():
-            grads_last(u - LAG_LAST)
+            last(u - LAG_LAST)
 
     for u in range(AHEAD_PASS):
         pass_on(u)
@@ -279,21 +295,18 @@
         return carry
 
     lax.fori_loop(0, KVH, step, 0)
-    grads_mate_straight(units - 1)
-    each(units - LAG_PASS, units - STRAIGHT, grads_pass)
+    merge(units - 1)
+    each(units - LAG_PASS, units - STRAIGHT_LAST, grads_pass)
     each(0, KVH, query_phase)
-    each(units - LAG_LAST, units - STRAIGHT, grads_last)
-    each(units - STRAIGHT, units, grads_last_straight)
-    for g in range(KVH):
-        cols = slice(g * HD, (g + 1) * HD)
-        dv_ref[:, cols] = own[2 * g, 0:tok].astype(bf16)
-        dk_ref[:, cols] = own[2 * g + 1, 0:tok].astype(bf16)
-
-    def finish(u):
-        for copy in (near, far, share, pair, back_far, back_near):
+
+    def sent(u):
+        for copy in (near, far, share, pair, back_far):
             copy(u).wait_send()
 
-    each(0, units, finish)
+    each(0, units, sent)
+    each(0, units - STRAIGHT_LAST, lambda u: back_near(u).wait_send())
+    each(units - LAG_LAST, units, last)
+    each(units - STRAIGHT_LAST, units, lambda u: back_near(u).wait_send())
 
 
 def out_kernel(dq_in, dk_in, dv_in, dq, dk, dv, sems):

time: 52.3 us -> 49.8 us (0.952)
  Pallas kernels: 51.6 us -> 49.1 us
    pallas_call x1, Pallas kernels: 50 us -> 47.5 us  [per_device(): pl.pallas_call(kernel, out_shape=(pltpu.VMEM((KVH, tok, GW), bf16), pltpu...]
where the time goes in v3:
time: 49.8 us
  Pallas kernels  49.1 us (99%)
  between operations  0.64 us (1%)
    pallas_call x1, Pallas kernels, per_device(): pl.pallas_call(kernel, out_shape=(pltpu.VMEM((KVH, tok, GW), bf16), pltpu...  47.5 us
    pallas_call x1, Pallas kernels, finish_out(): pl.pallas_call(out_kernel, out_shape=(jax.ShapeDtypeStruct((tok, groups *...  1.57 us

profile of v3, /device:TPU:1, one launch (start us, length us, event | category | flops | bytes accessed | tf_op | source)
XLA Modules:
  0.0 49.8 jit_solution(10067089060299625990)
XLA Ops:
  0.6 47.5 %shard_map.103 = (bf16[8,128,1024]{2,1,0:T(8,128)(2,1)S(1)}, bf16[128,1024]{1,0:T(8,128)(2,1)S(1)}, bf16[128,1024]{1,0:T(8,128)(2,1)S(1)}) custom-call(s32[8]{0:T(128)} %starts.1, f32[8]{0:T(128)} %weights.1, bf16[128,8192]{1,0:T(8,128)(2,1)} %q_hbm.1, bf16[128,8192]{1,0:T(8,128)(2,1)} %do_hbm.1, bf16[128,8192]{1,0:T(8,128)(2,1)} %o_hbm.1, ...), custom_call_target="tpu_custom_call" | custom-call | flops 6710886400 | bytes 9437184 | tf_op jit(solution)/shard_map/pallas_call | solution.py:357
  48.2 1.6 %shard_map.104 = (bf16[128,8192]{1,0:T(8,128)(2,1)}, bf16[128,1024]{1,0:T(8,128)(2,1)}, bf16[128,1024]{1,0:T(8,128)(2,1)}) custom-call(bf16[8,128,1024]{2,1,0:T(8,128)(2,1)S(1)} %get-tuple-element.6.dq_in, bf16[128,1024]{1,0:T(8,128)(2,1)S(1)} %get-tuple-element.7.dk_in, bf16[128,1024]{1,0:T(8,128)(2,1)S(1)} %get-tuple-element.8.dv_in), custom_call_target="tpu_custom_call" | custom-call | tf_op jit(solution)/shard_map/pallas_call | solution.py:330

commit v4 on v3

--- a/solution.py
+++ b/solution.py
@@ -27,6 +27,7 @@
 LAG_LAST = 7
 STRAIGHT_FIRST = 0
 STRAIGHT_LAST = 1
+GREET_TWO = 10
 
 
 def kernel(
@@ -99,9 +100,12 @@
         lax.fori_loop(lo, hi, step, 0)
 
     barrier = pltpu.get_barrier_semaphore()
-    partners = (up, down, mate, up_two, down_two)
-    for where in partners:
-        pl.semaphore_signal(barrier, inc=1, device_id=where, device_id_type=pl.DeviceIdType.MESH)
+
+    def greet(partners):
+        for where in partners:
+            pl.semaphore_signal(barrier, inc=1, device_id=where, device_id_type=pl.DeviceIdType.MESH)
+
+    greet((up, down, mate))
     for i in range(3):
         load_small(i).start()
     for i in (1, 2, 0):
@@ -111,7 +115,7 @@
     for g in range(KVH):
         kv[2 * g, 0:tok, :] = k_s[:, g * HD : (g + 1) * HD]
         kv[2 * g + 1, 0:tok, :] = v_s[:, g * HD : (g + 1) * HD]
-    pl.semaphore_wait(barrier, len(partners))
+    pl.semaphore_wait(barrier, 3)
     for u in range(AHEAD_PASS):
         near(u).start()
 
@@ -276,6 +280,10 @@
         def _():
             last(u - LAG_LAST)
 
+        @pl.when(u == GREET_TWO)
+        def _():
+            greet((up_two, down_two))
+
     for u in range(AHEAD_PASS):
         pass_on(u)
         if AHEAD_PASS + u < AHEAD_SEND:
@@ -295,6 +303,7 @@
         return carry
 
     lax.fori_loop(0, KVH, step, 0)
+    pl.semaphore_wait(barrier, 2)
     merge(units - 1)
     each(units - LAG_PASS, units - STRAIGHT_LAST, grads_pass)
     each(0, KVH, query_phase)

time: 49.8 us -> 49.3 us (0.990)
  Pallas kernels: 49.1 us -> 48.5 us
    pallas_call x1, Pallas kernels: 47.5 us -> 47 us  [per_device(): pl.pallas_call(kernel, out_shape=(pltpu.VMEM((KVH, tok, GW), bf16), pltpu...]
where the time goes in v4:
time: 49.3 us; the launch traced here: 49.2 us
  Pallas kernels  48.5 us (98%)
  between operations  0.64 us (1%)
    pallas_call x1, Pallas kernels, per_device(): pl.pallas_call(kernel, out_shape=(pltpu.VMEM((KVH, tok, GW), bf16), pltpu...  47 us
    pallas_call x1, Pallas kernels, finish_out(): pl.pallas_call(out_kernel, out_shape=(jax.ShapeDtypeStruct((tok, groups *...  1.57 us

profile of v4, /device:TPU:1, one launch (start us, length us, event | category | flops | bytes accessed | tf_op | source)
XLA Modules:
  0.0 49.2 jit_solution(11293196377009473074)
XLA Ops:
  0.6 47.0 %shard_map.103 = (bf16[8,128,1024]{2,1,0:T(8,128)(2,1)S(1)}, bf16[128,1024]{1,0:T(8,128)(2,1)S(1)}, bf16[128,1024]{1,0:T(8,128)(2,1)S(1)}) custom-call(s32[8]{0:T(128)} %starts.1, f32[8]{0:T(128)} %weights.1, bf16[128,8192]{1,0:T(8,128)(2,1)} %q_hbm.1, bf16[128,8192]{1,0:T(8,128)(2,1)} %do_hbm.1, bf16[128,8192]{1,0:T(8,128)(2,1)} %o_hbm.1, ...), custom_call_target="tpu_custom_call" | custom-call | flops 6710886400 | bytes 9437184 | tf_op jit(solution)/shard_map/pallas_call | solution.py:366
  47.6 1.6 %shard_map.104 = (bf16[128,8192]{1,0:T(8,128)(2,1)}, bf16[128,1024]{1,0:T(8,128)(2,1)}, bf16[128,1024]{1,0:T(8,128)(2,1)}) custom-call(bf16[8,128,1024]{2,1,0:T(8,128)(2,1)S(1)} %get-tuple-element.6.dq_in, bf16[128,1024]{1,0:T(8,128)(2,1)S(1)} %get-tuple-element.7.dk_in, bf16[128,1024]{1,0:T(8,128)(2,1)S(1)} %get-tuple-element.8.dv_in), custom_call_target="tpu_custom_call" | custom-call | tf_op jit(solution)/shard_map/pallas_call | solution.py:339

commit v5 on v4

--- a/solution.py
+++ b/solution.py
@@ -24,7 +24,7 @@
 AHEAD_PASS = 5
 AHEAD_PAIR = 2
 LAG_PASS = 4
-LAG_LAST = 7
+LAG_LAST = 8
 STRAIGHT_FIRST = 0
 STRAIGHT_LAST = 1
 GREET_TWO = 10
@@ -305,8 +305,10 @@
     lax.fori_loop(0, KVH, step, 0)
     pl.semaphore_wait(barrier, 2)
     merge(units - 1)
-    each(units - LAG_PASS, units - STRAIGHT_LAST, grads_pass)
-    each(0, KVH, query_phase)
+    each(units - LAG_PASS, units - STRAIGHT_LAST - 1, grads_pass)
+    each(0, KVH // 2, query_phase)
+    grads_pass(units - STRAIGHT_LAST - 1)
+    each(KVH // 2, KVH, query_phase)
 
     def sent(u):
         for copy in (near, far, share, pair, back_far):

time: 49.3 us -> 49.3 us (level)
  no operation moved by 1% of the time
where the time goes in v5:
time: 49.3 us; the launch traced here: 49.2 us
  Pallas kernels  48.5 us (98%)
  between operations  0.64 us (1%)
    pallas_call x1, Pallas kernels, per_device(): pl.pallas_call(kernel, out_shape=(pltpu.VMEM((KVH, tok, GW), bf16), pltpu...  47 us
    pallas_call x1, Pallas kernels, finish_out(): pl.pallas_call(out_kernel, out_shape=(jax.ShapeDtypeStruct((tok, groups *...  1.57 us

profile of v5, /device:TPU:1, one launch (start us, length us, event | category | flops | bytes accessed | tf_op | source)
XLA Modules:
  0.0 49.2 jit_solution(4042541330204875652)
XLA Ops:
  0.6 47.0 %shard_map.103 = (bf16[8,128,1024]{2,1,0:T(8,128)(2,1)S(1)}, bf16[128,1024]{1,0:T(8,128)(2,1)S(1)}, bf16[128,1024]{1,0:T(8,128)(2,1)S(1)}) custom-call(s32[8]{0:T(128)} %starts.1, f32[8]{0:T(128)} %weights.1, bf16[128,8192]{1,0:T(8,128)(2,1)} %q_hbm.1, bf16[128,8192]{1,0:T(8,128)(2,1)} %do_hbm.1, bf16[128,8192]{1,0:T(8,128)(2,1)} %o_hbm.1, ...), custom_call_target="tpu_custom_call" | custom-call | flops 6710886400 | bytes 9437184 | tf_op jit(solution)/shard_map/pallas_call | solution.py:368
  47.6 1.6 %shard_map.104 = (bf16[128,8192]{1,0:T(8,128)(2,1)}, bf16[128,1024]{1,0:T(8,128)(2,1)}, bf16[128,1024]{1,0:T(8,128)(2,1)}) custom-call(bf16[8,128,1024]{2,1,0:T(8,128)(2,1)S(1)} %get-tuple-element.6.dq_in, bf16[128,1024]{1,0:T(8,128)(2,1)S(1)} %get-tuple-element.7.dk_in, bf16[128,1024]{1,0:T(8,128)(2,1)S(1)} %get-tuple-element.8.dv_in), custom_call_target="tpu_custom_call" | custom-call | tf_op jit(solution)/shard_map/pallas_call | solution.py:341
